TPU v7x, 32 devices: a whole 2x2x4 slice. The times are simulated.
32 devices in a mesh: win: 8 (over y, x, core), row: 4 (over z).
Axes of the slice: x: 2, y: 2, z: 4, core: 2. Of those that a mesh axis runs over, the one named last changes fastest.
Arguments:
- downgoing: float32 [8, 3072, 3072], P('win', 'row'), may hold values from -64 to 64
- upgoing: float32 [8, 64, 3072], P('win'), may hold values from -6 to 6
Outputs:
- filters: float32 [32, 2, 64, 3072], P('win', None, None, 'row')
All inputs are finite; a program needn't handle non-finite values.
Results may differ from a plain program's by a relative error of at most 0.00016.
Values sent between devices are 32-bit elements; how exact they have to be, the bound alone decides.
A program may use at most 128 MiB of HBM per device.

v0:
```python
import math

import jax
import jax.numpy as jnp
from jax import lax
from jax.sharding import PartitionSpec as P

NCH = 3072
FREQ_DEV = 4
ITERS = 2


damping = 0.5


def dft_table(n_samples, n_bins):
    sample_idx = jnp.arange(n_samples, dtype=jnp.int32)
    bin_idx = jnp.arange(1, n_bins + 1, dtype=jnp.int32)
    angles = (sample_idx[:, None] * bin_idx[None, :] % n_samples).astype(jnp.float32) * (
        2.0 * math.pi / n_samples
    )
    return jnp.concatenate([jnp.cos(angles), -jnp.sin(angles)], axis=1) * (
        1.0 / math.sqrt(n_samples)
    )


def contract(pattern, first, second):
    return jnp.einsum(
        pattern, first, second, precision=lax.Precision.HIGHEST, preferred_element_type=jnp.float32
    )


def cg_solve(down_re, down_im, up_re, up_im):
    root_chan = math.sqrt(NCH)
    rhs_re = (
        contract("kwv,kwc->kvc", up_re, down_re) + contract("kwv,kwc->kvc", up_im, down_im)
    ) / root_chan
    rhs_im = (
        contract("kwv,kwc->kvc", up_im, down_re) - contract("kwv,kwc->kvc", up_re, down_im)
    ) / root_chan

    def residual_total(res_re, res_im):
        partial_sum = jnp.sum(res_re * res_re + res_im * res_im, axis=-1, keepdims=True)
        return lax.psum(partial_sum, "row")

    filt_re = jnp.zeros_like(rhs_re)
    filt_im = jnp.zeros_like(rhs_im)
    res_re, res_im = (rhs_re, rhs_im)
    dir_re, dir_im = (rhs_re, rhs_im)
    norm_old = residual_total(res_re, res_im)
    for iteration in range(ITERS):
        sum_re = contract("kvc,kwc->kvw", dir_re, down_re) - contract(
            "kvc,kwc->kvw", dir_im, down_im
        )
        sum_im = contract("kvc,kwc->kvw", dir_re, down_im) + contract(
            "kvc,kwc->kvw", dir_im, down_re
        )
        sum_re, sum_im = lax.psum((sum_re, sum_im), "row")
        img_re = (
            contract("kvw,kwc->kvc", sum_re, down_re) + contract("kvw,kwc->kvc", sum_im, down_im)
        ) / NCH + damping * dir_re
        img_im = (
            contract("kvw,kwc->kvc", sum_im, down_re) - contract("kvw,kwc->kvc", sum_re, down_im)
        ) / NCH + damping * dir_im
        operate_partial_sum = jnp.sum(dir_re * img_re + dir_im * img_im, axis=-1, keepdims=True)
        curvature = lax.psum(operate_partial_sum, "row")
        img_re, img_im, curvature = (img_re, img_im, curvature)
        step_size = norm_old / curvature
        filt_re = filt_re + step_size * dir_re
        filt_im = filt_im + step_size * dir_im
        res_re = res_re - step_size * img_re
        res_im = res_im - step_size * img_im
        norm_new = residual_total(res_re, res_im)
        ratio = norm_new / norm_old
        dir_re = res_re + ratio * dir_re
        dir_im = res_im + ratio * dir_im
        norm_old = norm_new
    out_scale = math.sqrt(NCH / down_re.shape[1])
    return (filt_re * out_scale, filt_im * out_scale)


def body(downgoing, upgoing):
    n_samples = downgoing.shape[2]
    n_owners = lax.axis_size("win")
    n_bins = FREQ_DEV * n_owners
    basis = dft_table(n_samples, n_bins)
    spec_down = contract("wct,tk->wkc", downgoing, basis)
    spec_down = spec_down.reshape(downgoing.shape[0], 2, n_owners, FREQ_DEV, downgoing.shape[1])
    spec_up = contract("wct,tk->wkc", upgoing, basis)
    spec_up = spec_up.reshape(upgoing.shape[0], 2, n_owners, FREQ_DEV, upgoing.shape[1])
    down_spec = jnp.moveaxis(
        lax.all_to_all(spec_down, "win", split_axis=2, concat_axis=0, tiled=True)[:, :, 0], 2, 0
    )
    up_spec = jnp.moveaxis(
        lax.all_to_all(spec_up, "win", split_axis=2, concat_axis=0, tiled=True)[:, :, 0], 2, 0
    )
    filt_re, filt_im = cg_solve(
        down_spec[:, :, 0], down_spec[:, :, 1], up_spec[:, :, 0], up_spec[:, :, 1]
    )
    return jnp.stack([filt_re, filt_im], axis=1)


def solution(mesh):
    in_specs = (P("win", "row", None), P("win", None, None))
    out_specs = P("win", None, None, "row")
    return jax.shard_map(body, mesh=mesh, in_specs=in_specs, out_specs=out_specs, check_vma=False)
```

profile of v0, /device:TPU:0, one launch (start us, length us, event | category | flops | bytes accessed | tf_op | source)
XLA Modules:
  0.0 120.5 jit_solution(1688204488254332392)
XLA Ops:
  0.0 0.0 copy-start
  0.0 1.7 %fusion.33 = (f32[3072,32]{0,1:T(8,128)S(1)}, f32[3072,32]{0,1:T(8,128)S(1)}) fusion(s32[32]{0:T(128)S(1)} %iota_add_fusion), kind=kLoop, calls=%fused_computation.56 | loop fusion | flops 983040 | bytes 786560 | tf_op jit(solution)/shard_map/cos | solution.py:22
  1.7 0.1 fusion.17
  1.8 0.2 reshape.28
  2.0 0.0 copy-done
  2.0 1.2 convolution_bitcast_fusion
  3.2 0.7 reshape.33
  3.9 5.2 %all-to-all-start = ((f32[8,1,512]{2,1,0:T(1,128)}), f32[8,1,512]{2,1,0:T(1,128)S(1)}, u32[]{:S(2)}, u32[]{:S(2)}) async-start(f32[8,1,512]{2,1,0:T(1,128)} %reshape.33), calls=%async_computation | async-start | bytes 32768 | tf_op jit(solution)/shard_map/all_to_all | solution.py:95
  9.0 12.3 %fusion.14 = f32[1,2,8,4,768]{4,3,2,1,0:T(4,128)S(1)} fusion(f32[2,8,4,3072]{3,2,1,0:T(4,128)S(1)} %reshape.28, f32[1,768,3072]{2,1,0:T(8,128)} %param.2), kind=kOutput, calls=%fused_computation.21 | convolution fusion | flops 1811939328 | bytes 10420224 | tf_op jit(solution)/shard_map/wct,tk->wkc/dot_general | solution.py:28
  21.4 0.7 copy.9
  22.1 0.0 all-to-all-done
  22.1 4.2 %all-to-all-start.1 = ((f32[1,2,8,4,768]{4,3,1,0,2:T(4,128)}), f32[1,2,8,4,768]{4,3,1,0,2:T(4,128)S(1)}, u32[]{:S(2)}, u32[]{:S(2)}) async-start(f32[1,2,8,4,768]{4,3,1,0,2:T(4,128)} %copy.9), calls=%async_computation.1 | async-start | bytes 393216 | tf_op jit(solution)/shard_map/all_to_all | solution.py:92
  26.3 0.6 broadcast.69
  26.8 0.7 reduce
  27.6 0.1 reshape.34
  27.7 4.8 %all-to-all-done.1 = f32[1,2,8,4,768]{4,3,1,0,2:T(4,128)S(1)} async-done(((f32[1,2,8,4,768]{4,3,1,0,2:T(4,128)}), f32[1,2,8,4,768]{4,3,1,0,2:T(4,128)S(1)}, u32[]{:S(2)}, u32[]{:S(2)}) %all-to-all-start.1) | async-done | bytes 196640 | tf_op jit(solution)/shard_map/all_to_all | solution.py:92
  32.5 0.1 copy.17
  32.6 0.8 fusion.40
  33.4 0.8 fusion.41
  34.2 0.8 convolution_add_fusion.2
  35.0 0.8 fusion.21
  35.8 0.8 fusion.23
  36.6 0.8 convolution_subtract_fusion.2
  37.4 0.8 convolution_add_fusion.4
  38.2 0.8 convolution_subtract_fusion.4
  39.0 19.3 %all-reduce.2 = (f32[4,64,8]{1,2,0:T(8,128)S(1)}, f32[4,64,8]{1,2,0:T(8,128)S(1)}) all-reduce(f32[4,64,8]{1,2,0:T(8,128)S(1)} %convolution_add_fusion.4, f32[4,64,8]{1,2,0:T(8,128)S(1)} %convolution_subtract_fusion.4), channel_id=1, replica_groups=mesh['win'=8,'row'=4] {'row'}, use_global_device_ids=true, to_apply=%region_3.4 | all-reduce | flops 4096 | bytes 32768 | tf_op jit(solution)/shard_map/psum | solution.py:58
  58.3 0.8 fusion.38
  59.1 0.8 fusion.39
  59.9 0.9 fusion.12
  60.8 0.0 copy-start.3
  60.8 2.0 %add_reduce_fusion.1 = (f32[4,64]{1,0:T(4,128)S(1)}, f32[4,64]{1,0:T(4,128)S(1)}, f32[4,64,768]{2,1,0:T(8,128)}) fusion(f32[4,64,768]{2,1,0:T(8,128)S(1)} %fusion.12, f32[4,64,768]{2,1,0:T(8,128)S(1)} %convolution_subtract_fusion.2, f32[4,64,768]{2,1,0:T(8,128)S(1)} %convolution_add_fusion.2, f32[4,64,768]{2,1,0:T(8,128)S(1)} %fusion.38, ...), kind=kOutput, calls=%fused_computation.37 | convolution fusion | flops 21626368 | bytes 4048896 | tf_op jit(solution)/shard_map/kvw,kwc->kvc/dot_general | solution.py:28
  62.9 8.3 %all-reduce.1 = (f32[4,64,1]{1,0,2:T(4,128)S(1)}, f32[4,64,1]{1,0,2:T(4,128)S(1)}) all-reduce(f32[4,64,1]{1,0,2:T(4,128)S(1)} %bitcast.134, f32[4,64,1]{1,0,2:T(4,128)S(1)} %bitcast.133), channel_id=1, replica_groups=mesh['win'=8,'row'=4] {'row'}, use_global_device_ids=true, to_apply=%region_1.2 | all-reduce | flops 512 | bytes 4096 | tf_op jit(solution)/shard_map/psum | solution.py:44
  71.2 0.0 copy-done.3
  71.2 1.5 %add_reduce_fusion = f32[4,64]{1,0:T(4,128)S(1)} fusion(f32[4,64,768]{2,1,0:T(8,128)} %get-tuple-element.21, f32[4,64,768]{2,1,0:T(8,128)S(1)} %convolution_subtract_fusion.2, f32[4,64,768]{2,1,0:T(8,128)S(1)} %fusion.12, f32[4,64,768]{2,1,0:T(8,128)S(1)} %convolution_add_fusion.2, f32[4,64]{1,0:T(4,128)S(1)} %get-tuple-element.14), kind=kLoop, calls=%fused_computation.34 | loop fusion | flops 1965824 | bytes 3147776 | tf_op jit(solution)/shard_map/reduce_sum | solution.py:43
  72.8 10.4 %psum.60 = f32[4,64,1]{1,0,2:T(4,128)S(1)} all-reduce(f32[4,64,1]{1,0,2:T(4,128)S(1)} %bitcast.135), channel_id=1, replica_groups=mesh['win'=8,'row'=4] {'row'}, use_global_device_ids=true, to_apply=%region_7.8 | all-reduce | flops 256 | bytes 2048 | tf_op jit(solution)/shard_map/psum | solution.py:44
  83.1 1.7 %multiply_add_fusion.1 = (f32[4,64,768]{2,1,0:T(8,128)S(1)}, f32[4,64,768]{2,1,0:T(8,128)S(1)}) fusion(f32[4,64,768]{2,1,0:T(8,128)S(1)} %convolution_add_fusion.2, f32[4,64,768]{2,1,0:T(8,128)} %copy-done.3, f32[4,64]{1,0:T(4,128)S(1)} %multiply_bitcast_fusion.2, f32[4,64]{1,0:T(4,128)S(1)} %get-tuple-element.14, ...), kind=kLoop, calls=%fused_computation.33 | loop fusion | flops 1966080 | bytes 4720640 | tf_op jit(solution)/shard_map/add | solution.py:75
  84.9 0.0 copy-start.1
  84.9 0.8 fusion.42
  85.6 0.8 fusion.37
  86.4 0.8 convolution_add_fusion.3
  87.2 0.0 copy-done.1
  87.2 0.8 convolution_subtract_fusion.3
  88.0 16.0 %all-reduce = (f32[4,64,8]{1,2,0:T(8,128)S(1)}, f32[4,64,8]{1,2,0:T(8,128)S(1)}) all-reduce(f32[4,64,8]{1,2,0:T(8,128)S(1)} %convolution_subtract_fusion.3, f32[4,64,8]{1,2,0:T(8,128)S(1)} %convolution_add_fusion.3), channel_id=1, replica_groups=mesh['win'=8,'row'=4] {'row'}, use_global_device_ids=true, to_apply=%region_8.9 | all-reduce | flops 4096 | bytes 32768 | tf_op jit(solution)/shard_map/psum | solution.py:58
  104.0 0.8 fusion.36
  104.8 0.0 copy-start.2
  104.8 0.8 fusion.35
  105.7 0.9 fusion.8
  106.6 0.0 copy-done.2
  106.6 1.0 fusion.13
  107.6 10.0 %psum.63 = f32[4,64,1]{1,0,2:T(4,128)S(1)} all-reduce(f32[4,64,1]{1,0,2:T(4,128)S(1)} %bitcast.136), channel_id=1, replica_groups=mesh['win'=8,'row'=4] {'row'}, use_global_device_ids=true, to_apply=%region_11.12 | all-reduce | flops 256 | bytes 2048 | tf_op jit(solution)/shard_map/psum | solution.py:66
  117.7 1.4 %multiply_bitcast_fusion.1 = (f32[4,1,64,768]{3,2,0,1:T(8,128)S(1)}, f32[4,1,64,768]{3,2,0,1:T(8,128)S(1)}) fusion(f32[4,64,768]{2,1,0:T(8,128)S(1)} %get-tuple-element.17, f32[4,64,768]{2,1,0:T(8,128)S(1)} %convolution_add_fusion.2, f32[4,64]{1,0:T(4,128)S(1)} %divide_bitcast_fusion, f32[4,64]{1,0:T(4,128)S(1)} %get-tuple-element.13, ...), kind=kLoop, calls=%fused_computation.31 | loop fusion | flops 1572864 | bytes 4720640 | tf_op jit(solution)/shard_map/stack | solution.py:100
  119.1 0.2 pad_maximum_fusion
  119.2 1.3 %copy.11 = f32[4,2,64,768]{3,2,1,0:T(8,128)} copy(f32[4,2,64,768]{3,2,0,1:T(8,128)S(1)} %pad_maximum_fusion) | data formatting | bytes 3145728 | tf_op jit(solution)/shard_map/stack | solution.py:100
  (6 shorter events, 0.0 us)
Async XLA Ops:
  0.0 2.0 %copy-start = (f32[1,64,3072]{2,1,0:T(8,128)S(1)}, f32[1,64,3072]{2,1,0:T(8,128)}, u32[]{:S(2)}) copy-start(f32[1,64,3072]{2,1,0:T(8,128)} %param.3) | copy-start | bytes 2359300
  3.9 18.2 %all-to-all-start = ((f32[8,1,512]{2,1,0:T(1,128)}), f32[8,1,512]{2,1,0:T(1,128)S(1)}, u32[]{:S(2)}, u32[]{:S(2)}) async-start(f32[8,1,512]{2,1,0:T(1,128)} %reshape.33), calls=%async_computation | async-start | bytes 32768 | tf_op jit(solution)/shard_map/all_to_all | solution.py:95
  22.1 10.4 %all-to-all-start.1 = ((f32[1,2,8,4,768]{4,3,1,0,2:T(4,128)}), f32[1,2,8,4,768]{4,3,1,0,2:T(4,128)S(1)}, u32[]{:S(2)}, u32[]{:S(2)}) async-start(f32[1,2,8,4,768]{4,3,1,0,2:T(4,128)} %copy.9), calls=%async_computation.1 | async-start | bytes 393216 | tf_op jit(solution)/shard_map/all_to_all | solution.py:92
  60.8 10.4 %copy-start.3 = (f32[4,64,768]{2,1,0:T(8,128)}, f32[4,64,768]{2,1,0:T(8,128)S(1)}, u32[]{:S(2)}) copy-start(f32[4,64,768]{2,1,0:T(8,128)S(1)} %fusion.12) | copy-start | bytes 2359300
  84.9 2.3 %copy-start.1 = (f32[4,64,768]{2,1,0:T(8,128)}, f32[4,64,768]{2,1,0:T(8,128)S(1)}, u32[]{:S(2)}) copy-start(f32[4,64,768]{2,1,0:T(8,128)S(1)} %get-tuple-element.18) | copy-start | bytes 2359300
  104.8 1.8 %copy-start.2 = (f32[4,64,768]{2,1,0:T(8,128)S(1)}, f32[4,64,768]{2,1,0:T(8,128)}, u32[]{:S(2)}) copy-start(f32[4,64,768]{2,1,0:T(8,128)} %copy-done.1) | copy-start | bytes 2359300
where the time goes:
time: 121 us
  blocking collectives  64 us (53%)
  matrix products  31.1 us (26%)
  starting transfers between devices  9.37 us (8%)
  other arithmetic  7.33 us (6%)
  waiting for transfers between devices  4.81 us (4%)
  local copies, waits for them, and re-layouts  3.65 us (3%)
    psum x2, blocking collectives, cg_solve(): sum_re, sum_im = lax.psum((sum_re, sum_im), 'row')  35.3 us
    dot_general x22, matrix products, contract(): jnp.einsum(pattern, first, second, precision=lax.Precision.HIGHEST, prefe...  31.1 us
    psum x2, blocking collectives, residual_total(): return lax.psum(partial_sum, 'row')  18.7 us
    psum x1, blocking collectives, cg_solve(): curvature = lax.psum(operate_partial_sum, 'row')  10 us
    all_to_all x1, starting transfers between devices, body(): lax.all_to_all(spec_up, 'win', split_axis=2, concat_axis=0, tiled=True)  5.17 us
    all_to_all x1, waiting for transfers between devices, body(): lax.all_to_all(spec_down, 'win', split_axis=2, concat_axis=0, tiled=True)  4.81 us
    all_to_all x1, starting transfers between devices, body(): lax.all_to_all(spec_down, 'win', split_axis=2, concat_axis=0, tiled=True)  4.2 us
  transfers between devices with their start and end apart: 2, of which 1 were waited for; matrix products, arithmetic and copies ran while one was open for 12% of the time, Pallas kernels for 0%

commit v1 on v0

v1 whole, which is shorter than its diff:
```python
import functools
import math

import jax
import jax.numpy as jnp
import numpy as np
from jax import lax
from jax.experimental import pallas as pl
from jax.experimental.pallas import tpu as pltpu
from jax.sharding import PartitionSpec as P

FREQ_DEV = 4
ITERS = 2
DAMPING = 0.5
LANES = 128
MESH = pl.DeviceIdType.MESH
F32, BF16 = jnp.float32, jnp.bfloat16


def dft_table(n_samples, n_bins):
    angles = (np.arange(n_samples)[:, None] * np.arange(1, n_bins + 1)[None, :] % n_samples) * (
        2.0 * math.pi / n_samples
    )
    table = np.stack([np.cos(angles), -np.sin(angles)], axis=2).reshape(n_samples, 2 * n_bins)
    table = (table / math.sqrt(n_samples)).astype(np.float32)
    head = table.astype(BF16)
    tail = (table - head.astype(np.float32)).astype(BF16)
    return np.concatenate([head, tail], axis=1)


def halves(value):
    head = value.astype(BF16)
    return head, (value - head.astype(F32)).astype(BF16)


def dot(first, second, dims):
    return lax.dot_general(first, second, (dims, ((), ())), preferred_element_type=F32)


def spectra(series, table):
    m, n_samples = series.shape
    step = 256
    total = None
    for at in range(0, n_samples, step):
        head, tail = halves(series[:, at : at + step])
        part = dot(jnp.concatenate([head, tail], axis=0), table[at : at + step, :], ((1,), (0,)))
        part = part[:m] + part[m:]
        total = part if total is None else total + part
    if m % LANES:
        total = jnp.concatenate([total, jnp.zeros((LANES - m % LANES, total.shape[1]), F32)], axis=0)
    total = total.T
    n = total.shape[0] // 2
    return total[:n] + total[n:]


def solve(rhs, gram, n_freq, n_chan, scale):
    rows, n_virt = rhs.shape

    head, tail = halves(gram)
    operator = jnp.concatenate([head, head, tail], axis=1)

    def project(coef):
        c_head, c_tail = halves(coef)
        return dot(operator, jnp.concatenate([c_head, c_tail, c_head], axis=0), ((1,), (0,)))

    def inner(one, two):
        prod = (one * two).reshape(n_freq, rows // n_freq, n_virt)
        total = jnp.sum(prod, axis=1, keepdims=True)
        return jnp.broadcast_to(total, prod.shape).reshape(rows, n_virt)

    filt = jnp.zeros_like(rhs)
    resid, direc = rhs, rhs
    resid_g = project(resid)
    direc_g = resid_g
    norm_old = inner(resid, resid_g)
    for iteration in range(ITERS):
        image = direc_g / n_chan + DAMPING * direc
        curvature = inner(direc_g, image)
        step = norm_old / curvature
        filt = filt + step * direc
        if iteration + 1 < ITERS:
            resid = resid - step * image
            resid_g = resid_g - step * project(image)
            norm_new = inner(resid, resid_g)
            ratio = norm_new / norm_old
            direc = resid + ratio * direc
            direc_g = resid_g + ratio * direc_g
            norm_old = norm_new
    return filt * scale


def solve_kernel(
    dims, x_hbm, up_hbm, tab_hbm, eh_out, el_out, y_out,
    xv, upv, tab, sbuf, ubuf, recv, urecv, eh, el, g_send, g_recv,
    in_sem, send_sem, recv_sem, g_sem, out_sem,
):
    n_win, n_row, n_chunk, width, n_virt, n_chan = dims
    slab = 2 * FREQ_DEV
    rows = n_win * slab
    block = 2 * n_win
    me, row = lax.axis_index("win"), lax.axis_index("row")

    loads = [
        pltpu.make_async_copy(tab_hbm, tab, in_sem.at[0]),
        pltpu.make_async_copy(up_hbm.at[0], upv, in_sem.at[1]),
    ]
    for ch in range(n_chunk):
        loads.append(
            pltpu.make_async_copy(
                x_hbm.at[0, pl.ds(ch * width, width), :], xv.at[ch], in_sem.at[2 + ch]
            )
        )
    for load in loads:
        load.start()

    win_peers = [lax.rem(me + off, n_win) for off in range(1, n_win)]
    row_peers = [lax.rem(row + off, n_row) for off in range(1, n_row)]
    barrier = pltpu.get_barrier_semaphore()
    for peer in win_peers:
        pl.semaphore_signal(barrier, inc=1, device_id={"win": peer}, device_id_type=MESH)
    for peer in row_peers:
        pl.semaphore_signal(barrier, inc=1, device_id={"row": peer}, device_id_type=MESH)

    def share(src, dst, at):
        own = pl.ds(pl.multiple_of(me * slab, slab), slab)
        dst[:, own, :] = src[:, own, :]
        for peer in win_peers:
            pltpu.make_async_remote_copy(
                src_ref=src.at[:, pl.ds(pl.multiple_of(peer * slab, slab), slab), :],
                dst_ref=dst.at[:, own, :],
                send_sem=send_sem.at[at],
                recv_sem=recv_sem.at[at],
                device_id={"win": peer},
                device_id_type=MESH,
            ).start()

    def put(dst, value):
        for sub in range(dst.shape[0]):
            dst[sub] = value[:, sub * LANES : (sub + 1) * LANES]

    def gather(src, number):
        parts = [src[sub, pl.ds(number, n_win, stride=slab), :] for sub in range(src.shape[0])]
        return jnp.concatenate(parts, axis=1) if len(parts) > 1 else parts[0]

    def await_all(ref, sem):
        part = ref.at[:, pl.ds(0, (n_win - 1) * slab), :]
        pltpu.make_async_copy(part, part, sem).wait()

    loads[0].wait()
    loads[1].wait()
    put(ubuf, spectra(upv, tab))
    pl.semaphore_wait(barrier, n_win + n_row - 2)
    share(ubuf, urecv, n_chunk)
    for ch in range(n_chunk):
        loads[2 + ch].wait()
        put(sbuf.at[ch], spectra(xv.at[ch], tab))
        share(sbuf.at[ch], recv.at[ch], ch)

    gram = None
    stores = []
    for ch in range(n_chunk):
        await_all(recv.at[ch], recv_sem.at[ch])
        left, right = [], []
        for f in range(FREQ_DEV):
            real = gather(recv.at[ch], 2 * f)
            imag = gather(recv.at[ch], 2 * f + 1)
            left += [real, imag]
            right += [-imag, real]
        ext = jnp.concatenate(
            [jnp.concatenate(left, axis=0), jnp.concatenate(right, axis=0)], axis=1
        )
        head, tail = halves(ext)
        eh[ch] = head
        el[ch] = tail
        for number, (src, dst) in enumerate(((eh, eh_out), (el, el_out))):
            store = pltpu.make_async_copy(src.at[ch], dst.at[ch], out_sem.at[2 * ch + number])
            store.start()
            stores.append(store)
        part = dot(
            jnp.concatenate([head, head, tail], axis=1),
            jnp.concatenate([head, tail, head], axis=1),
            ((1,), (1,)),
        )
        gram = part if gram is None else gram + part

    row_id = lax.broadcasted_iota(jnp.int32, (rows, rows), 0) // block
    col_id = lax.broadcasted_iota(jnp.int32, (rows, rows), 1) // block
    same_bin = row_id == col_id
    gram = jnp.where(same_bin, gram, 0.0)
    folded = gram[:block]
    for f in range(1, FREQ_DEV):
        folded = folded + gram[f * block : (f + 1) * block]
    packed = 2 * rows <= LANES
    if packed:
        folded = jnp.concatenate([folded[:n_win], folded[n_win:]], axis=1)
    g_send[...] = folded
    g_recv[row] = folded
    for off, peer in enumerate(row_peers):
        pltpu.make_async_remote_copy(
            src_ref=g_send,
            dst_ref=g_recv.at[row],
            send_sem=g_sem.at[0],
            recv_sem=g_sem.at[1],
            device_id={"row": peer},
            device_id_type=MESH,
        ).start()
    await_all(urecv, recv_sem.at[n_chunk])
    rhs = jnp.concatenate(
        [gather(urecv, number) for number in range(slab)], axis=0
    ) / math.sqrt(n_chan)
    rhs = rhs[:, :n_virt]
    if n_row > 1:
        part = g_recv.at[pl.ds(0, n_row - 1)]
        pltpu.make_async_copy(part, part, g_sem.at[1]).wait()
    folded = g_recv[0]
    for other in range(1, n_row):
        folded = folded + g_recv[other]
    if packed:
        folded = jnp.concatenate([folded[:, :rows], folded[:, rows:]], axis=0)
    gram = jnp.where(same_bin, jnp.concatenate([folded] * FREQ_DEV, axis=0), 0.0)
    y_out[...] = solve(rhs, gram, FREQ_DEV, n_chan, math.sqrt(n_chan / n_win))

    if n_row > 1:
        part = g_recv.at[pl.ds(0, n_row - 1)]
        pltpu.make_async_copy(part, part, g_sem.at[0]).wait()
    for ch in range(n_chunk):
        await_all(recv.at[ch], send_sem.at[ch])
    await_all(urecv, send_sem.at[n_chunk])
    for store in stores:
        store.wait()


def expand_kernel(dims, eh, el, y, out_hbm, ov, sem):
    n_win, n_chunk, width, n_virt = dims
    block = 2 * n_win
    stores = []
    for f in range(FREQ_DEV):
        own = slice(f * block, (f + 1) * block)
        head, tail = halves(y[own, :])
        coef = jnp.concatenate([head, tail, head], axis=0)
        for ch in range(n_chunk):
            big = eh[ch, own, :]
            part = dot(coef, jnp.concatenate([big, big, el[ch, own, :]], axis=0), ((0,), (0,)))
            span = slice(ch * width, (ch + 1) * width)
            ov[f, 0, :, span] = part[:, :width]
            ov[f, 1, :, span] = part[:, width:]
        store = pltpu.make_async_copy(ov.at[f], out_hbm.at[f], sem.at[f])
        store.start()
        stores.append(store)
    for store in stores:
        store.wait()


def body(downgoing, upgoing):
    _, n_local, n_samples = downgoing.shape
    n_virt = upgoing.shape[1]
    n_win, n_row = lax.axis_size("win"), lax.axis_size("row")
    n_chan = n_local * n_row
    width = 256 if n_local % 256 == 0 else 128
    n_chunk = n_local // width
    slab = 2 * FREQ_DEV
    rows = n_win * slab
    block = 2 * n_win
    table = jnp.asarray(dft_table(n_samples, FREQ_DEV * n_win))
    g_shape = (n_win, 2 * rows) if 2 * rows <= LANES else (block, rows)
    v_pad = -(-n_virt // LANES) * LANES
    dims = (n_win, n_row, n_chunk, width, n_virt, n_chan)
    any_spec = pl.BlockSpec(memory_space=pl.ANY)
    vmem_spec = pl.BlockSpec(memory_space=pltpu.VMEM)
    ext = jax.ShapeDtypeStruct((n_chunk, rows, 2 * width), BF16)
    eh, el, y = pl.pallas_call(
        functools.partial(solve_kernel, dims),
        out_shape=(ext, ext, jax.ShapeDtypeStruct((rows, n_virt), F32)),
        in_specs=[any_spec] * 3,
        out_specs=(any_spec, any_spec, vmem_spec),
        scratch_shapes=[
            pltpu.VMEM((n_chunk, width, n_samples), F32),
            pltpu.VMEM((n_virt, n_samples), F32),
            pltpu.VMEM(table.shape, BF16),
            pltpu.VMEM((n_chunk, width // LANES, rows, LANES), F32),
            pltpu.VMEM((v_pad // LANES, rows, LANES), F32),
            pltpu.VMEM((n_chunk, width // LANES, rows, LANES), F32),
            pltpu.VMEM((v_pad // LANES, rows, LANES), F32),
            pltpu.VMEM((n_chunk, rows, 2 * width), BF16),
            pltpu.VMEM((n_chunk, rows, 2 * width), BF16),
            pltpu.VMEM(g_shape, F32),
            pltpu.VMEM((n_row,) + g_shape, F32),
            pltpu.SemaphoreType.DMA((2 + n_chunk,)),
            pltpu.SemaphoreType.DMA((n_chunk + 1,)),
            pltpu.SemaphoreType.DMA((n_chunk + 1,)),
            pltpu.SemaphoreType.DMA((2,)),
            pltpu.SemaphoreType.DMA((2 * n_chunk,)),
        ],
        compiler_params=pltpu.CompilerParams(
            collective_id=0, has_side_effects=True, vmem_limit_bytes=50 * 1024 * 1024
        ),
        name="solve_bins",
    )(downgoing, upgoing, table)
    out_shape = (FREQ_DEV, 2, n_virt, n_local)
    return pl.pallas_call(
        functools.partial(expand_kernel, (n_win, n_chunk, width, n_virt)),
        out_shape=jax.ShapeDtypeStruct(out_shape, F32),
        in_specs=[vmem_spec] * 3,
        out_specs=any_spec,
        scratch_shapes=[pltpu.VMEM(out_shape, F32), pltpu.SemaphoreType.DMA((FREQ_DEV,))],
        compiler_params=pltpu.CompilerParams(vmem_limit_bytes=50 * 1024 * 1024),
        name="expand_bins",
    )(eh, el, y)


def solution(mesh):
    in_specs = (P("win", "row", None), P("win", None, None))
    out_specs = P("win", None, None, "row")
    return jax.shard_map(body, mesh=mesh, in_specs=in_specs, out_specs=out_specs, check_vma=False)
```

time: 121 us -> 22.7 us (0.19)
  blocking collectives: 64 us -> 0 us
  matrix products: 31.1 us -> 0 us
  Pallas kernels: 0 us -> 20.3 us
  starting transfers between devices: 9.37 us -> 0 us
  other arithmetic: 7.33 us -> 0 us
  waiting for transfers between devices: 4.81 us -> 0 us
  local copies, waits for them, and re-layouts: 3.65 us -> 2.27 us
    psum x5 -> x0, blocking collectives: 64 us -> none  [the longest x2 35.3 us: cg_solve(): sum_re, sum_im = lax.psum((sum_re, sum_im), 'row')]
    dot_general x22 -> x0, matrix products: 31.1 us -> none  [contract(): jnp.einsum(pattern, first, second, precision=lax.Precision.HIGHEST, prefe...]
    pallas_call x0 -> x2, Pallas kernels: none -> 20.3 us  [the longest x1 18.9 us: body(): pl.pallas_call(functools.partial(solve_kernel, dims), out_shape=(ext, ext...]
    all_to_all x2 -> x0, starting transfers between devices: 9.37 us -> none  [the longest x1 5.17 us: body(): lax.all_to_all(spec_up, 'win', split_axis=2, concat_axis=0, tiled=True)]
    all_to_all x2 -> x0, waiting for transfers between devices: 4.81 us -> none  [the longest x1 4.81 us: body(): lax.all_to_all(spec_down, 'win', split_axis=2, concat_axis=0, tiled=True)]
    add x2 -> x0, other arithmetic: 1.74 us -> none  [the longest x1 1.73 us: cg_solve(): dir_re = res_re + ratio * dir_re]
    cos x1 -> x0, other arithmetic: 1.67 us -> none  [dft_table(): jnp.cos(angles)]
    another operation x2 -> x0, other arithmetic: 1.57 us -> none  [body(): return jnp.stack([filt_re, filt_im], axis=1)]
  transfers between devices with their start and end apart: 2 -> 0, of which waited for: 1 -> 0; matrix products, arithmetic and copies ran while one was open for 12% -> 0% of each run, Pallas kernels for 0% -> 0%
where the time goes in v1:
time: 22.7 us; the launch traced here: 22.5 us
  Pallas kernels  20.3 us (89%)
  local copies, waits for them, and re-layouts  2.27 us (10%)
    pallas_call x1, Pallas kernels, body(): pl.pallas_call(functools.partial(solve_kernel, dims), out_shape=(ext, ext...  18.9 us
    unnamed x4, local copies, waits for them, and re-layouts  2.27 us
    pallas_call x1, Pallas kernels, body(): pl.pallas_call(functools.partial(expand_kernel, (n_win, n_chunk, width, n...  1.4 us

profile of v1, /device:TPU:0, one launch (start us, length us, event | category | flops | bytes accessed | tf_op | source)
XLA Modules:
  0.0 22.5 jit_solution(17076086368223543460)
XLA Ops:
  0.0 0.0 copy-start
  0.0 1.1 %copy-done = f32[1,64,3072]{2,1,0:T(8,128)S(1)} copy-done((f32[1,64,3072]{2,1,0:T(8,128)S(1)}, f32[1,64,3072]{2,1,0:T(8,128)}, u32[]{:S(2)}) %copy-start) | copy-done | bytes 786456
  1.1 0.0 copy-start.1
  1.1 1.1 %copy-done.1 = bf16[3072,128]{1,0:T(8,128)(2,1)S(1)} copy-done((bf16[3072,128]{1,0:T(8,128)(2,1)S(1)}, bf16[3072,128]{1,0:T(8,128)(2,1)}, u32[]{:S(2)}) %copy-start.1) | copy-done | bytes 786456
  2.3 18.9 %solve_bins.1 = (bf16[3,64,512]{2,1,0:T(8,128)(2,1)S(1)}, bf16[3,64,512]{2,1,0:T(8,128)(2,1)S(1)}, f32[64,64]{1,0:T(8,128)S(1)}) custom-call(f32[1,768,3072]{2,1,0:T(8,128)} %x_hbm.1, f32[1,64,3072]{2,1,0:T(8,128)S(1)} %copy-done, bf16[3072,128]{1,0:T(8,128)(2,1)S(1)} %copy-done.1), custom_call_target="tpu_custom_call" | custom-call | tf_op jit(solution)/shard_map/solve_bins/pallas_call | solution.py:271
  21.1 1.4 %expand_bins.1 = f32[4,2,64,768]{3,2,1,0:T(8,128)} custom-call(bf16[3,64,512]{2,1,0:T(8,128)(2,1)S(1)} %get-tuple-element.8.eh, bf16[3,64,512]{2,1,0:T(8,128)(2,1)S(1)} %get-tuple-element.9.el, f32[64,64]{1,0:T(8,128)S(1)} %get-tuple-element.10.y), custom_call_target="tpu_custom_call" | custom-call | tf_op jit(solution)/shard_map/expand_bins/pallas_call | solution.py:300
Async XLA Ops:
  0.0 1.1 %copy-start = (f32[1,64,3072]{2,1,0:T(8,128)S(1)}, f32[1,64,3072]{2,1,0:T(8,128)}, u32[]{:S(2)}) copy-start(f32[1,64,3072]{2,1,0:T(8,128)} %up_hbm.1) | copy-start | bytes 2359300
  1.1 1.1 %copy-start.1 = (bf16[3072,128]{1,0:T(8,128)(2,1)S(1)}, bf16[3072,128]{1,0:T(8,128)(2,1)}, u32[]{:S(2)}) copy-start(bf16[3072,128]{1,0:T(8,128)(2,1)} %constant.2.clone.tab_hbm) | copy-start | bytes 2359300

commit v2 on v1

--- a/solution.py
+++ b/solution.py
@@ -10,6 +10,8 @@
 from jax.sharding import PartitionSpec as P
 
 FREQ_DEV = 4
+PIECE = 1024
+AHEAD = 4
 ITERS = 2
 DAMPING = 0.5
 LANES = 128
@@ -37,15 +39,16 @@
     return lax.dot_general(first, second, (dims, ((), ())), preferred_element_type=F32)
 
 
-def spectra(series, table):
-    m, n_samples = series.shape
-    step = 256
-    total = None
-    for at in range(0, n_samples, step):
-        head, tail = halves(series[:, at : at + step])
-        part = dot(jnp.concatenate([head, tail], axis=0), table[at : at + step, :], ((1,), (0,)))
-        part = part[:m] + part[m:]
-        total = part if total is None else total + part
+def accumulate(total, series, table):
+    m = series.shape[0]
+    head, tail = halves(series)
+    part = dot(jnp.concatenate([head, tail], axis=0), table, ((1,), (0,)))
+    part = part[:m] + part[m:]
+    return part if total is None else total + part
+
+
+def by_bin(total):
+    m = total.shape[0]
     if m % LANES:
         total = jnp.concatenate([total, jnp.zeros((LANES - m % LANES, total.shape[1]), F32)], axis=0)
     total = total.T
@@ -100,18 +103,29 @@
     block = 2 * n_win
     me, row = lax.axis_index("win"), lax.axis_index("row")
 
-    loads = [
-        pltpu.make_async_copy(tab_hbm, tab, in_sem.at[0]),
-        pltpu.make_async_copy(up_hbm.at[0], upv, in_sem.at[1]),
-    ]
+    n_piece, piece = tab.shape[0], tab.shape[1]
+    loads, ready = [], []
     for ch in range(n_chunk):
-        loads.append(
-            pltpu.make_async_copy(
-                x_hbm.at[0, pl.ds(ch * width, width), :], xv.at[ch], in_sem.at[2 + ch]
-            )
-        )
-    for load in loads:
+        for k in range(n_piece):
+            span = pl.ds(k * piece, piece)
+            pairs = [(x_hbm.at[0, pl.ds(ch * width, width), span], xv.at[ch, k])]
+            if ch == 0:
+                pairs = [(tab_hbm.at[span, :], tab.at[k]), (up_hbm.at[0, :, span], upv.at[k])] + pairs
+            for src, dst in pairs:
+                loads.append(pltpu.make_async_copy(src, dst, in_sem.at[len(loads)]))
+            ready.append(len(loads))
+    ahead = 3 * AHEAD
+    for load in loads[:ahead]:
         load.start()
+    taken = [0]
+
+    def await_piece(number):
+        for at in range(taken[0], ready[number]):
+            loads[at].wait()
+        started = ahead + taken[0]
+        taken[0] = ready[number]
+        for load in loads[started : ahead + taken[0]]:
+            load.start()
 
     win_peers = [lax.rem(me + off, n_win) for off in range(1, n_win)]
     row_peers = [lax.rem(row + off, n_row) for off in range(1, n_row)]
@@ -146,15 +160,21 @@
         part = ref.at[:, pl.ds(0, (n_win - 1) * slab), :]
         pltpu.make_async_copy(part, part, sem).wait()
 
-    loads[0].wait()
-    loads[1].wait()
-    put(ubuf, spectra(upv, tab))
-    pl.semaphore_wait(barrier, n_win + n_row - 2)
-    share(ubuf, urecv, n_chunk)
     for ch in range(n_chunk):
-        loads[2 + ch].wait()
-        put(sbuf.at[ch], spectra(xv.at[ch], tab))
+        total = None
+        for k in range(n_piece):
+            await_piece(ch * n_piece + k)
+            series = xv[ch, k]
+            if ch == 0:
+                series = jnp.concatenate([series, upv[k]], axis=0)
+            total = accumulate(total, series, tab[k])
+        put(sbuf.at[ch], by_bin(total[:width]))
+        if ch == 0:
+            put(ubuf, by_bin(total[width:]))
+            pl.semaphore_wait(barrier, n_win + n_row - 2)
         share(sbuf.at[ch], recv.at[ch], ch)
+        if ch == 0:
+            share(ubuf, urecv, n_chunk)
 
     gram = None
     stores = []
@@ -258,6 +278,8 @@
     n_chan = n_local * n_row
     width = 256 if n_local % 256 == 0 else 128
     n_chunk = n_local // width
+    piece = PIECE if n_samples % PIECE == 0 else n_samples
+    n_piece = n_samples // piece
     slab = 2 * FREQ_DEV
     rows = n_win * slab
     block = 2 * n_win
@@ -271,12 +293,12 @@
     eh, el, y = pl.pallas_call(
         functools.partial(solve_kernel, dims),
         out_shape=(ext, ext, jax.ShapeDtypeStruct((rows, n_virt), F32)),
-        in_specs=[any_spec] * 3,
+        in_specs=[pl.BlockSpec(memory_space=pltpu.MemorySpace.HBM)] * 3,
         out_specs=(any_spec, any_spec, vmem_spec),
         scratch_shapes=[
-            pltpu.VMEM((n_chunk, width, n_samples), F32),
-            pltpu.VMEM((n_virt, n_samples), F32),
-            pltpu.VMEM(table.shape, BF16),
+            pltpu.VMEM((n_chunk, n_piece, width, piece), F32),
+            pltpu.VMEM((n_piece, n_virt, piece), F32),
+            pltpu.VMEM((n_piece, piece, table.shape[1]), BF16),
             pltpu.VMEM((n_chunk, width // LANES, rows, LANES), F32),
             pltpu.VMEM((v_pad // LANES, rows, LANES), F32),
             pltpu.VMEM((n_chunk, width // LANES, rows, LANES), F32),
@@ -285,7 +307,7 @@
             pltpu.VMEM((n_chunk, rows, 2 * width), BF16),
             pltpu.VMEM(g_shape, F32),
             pltpu.VMEM((n_row,) + g_shape, F32),
-            pltpu.SemaphoreType.DMA((2 + n_chunk,)),
+            pltpu.SemaphoreType.DMA(((2 + n_chunk) * n_piece,)),
             pltpu.SemaphoreType.DMA((n_chunk + 1,)),
             pltpu.SemaphoreType.DMA((n_chunk + 1,)),
             pltpu.SemaphoreType.DMA((2,)),

time: 22.7 us -> 23.4 us (1.031)
  Pallas kernels: 20.3 us -> 20.9 us
    pallas_call x1, Pallas kernels: 18.9 us -> 19.5 us  [body(): pl.pallas_call(functools.partial(solve_kernel, dims), out_shape=(ext, ext...]
where the time goes in v2:
time: 23.4 us; the launch traced here: 23.2 us
  Pallas kernels  20.9 us (89%)
  local copies, waits for them, and re-layouts  2.27 us (10%)
    pallas_call x1, Pallas kernels, body(): pl.pallas_call(functools.partial(solve_kernel, dims), out_shape=(ext, ext...  19.5 us
    unnamed x4, local copies, waits for them, and re-layouts  2.27 us
    pallas_call x1, Pallas kernels, body(): pl.pallas_call(functools.partial(expand_kernel, (n_win, n_chunk, width, n...  1.41 us

profile of v2, /device:TPU:0, one launch (start us, length us, event | category | flops | bytes accessed | tf_op | source)
XLA Modules:
  0.0 23.2 jit_solution(54114458119409175)
XLA Ops:
  0.0 0.0 copy-start
  0.0 1.1 %copy-done = f32[1,64,3072]{2,1,0:T(8,128)S(1)} copy-done((f32[1,64,3072]{2,1,0:T(8,128)S(1)}, f32[1,64,3072]{2,1,0:T(8,128)}, u32[]{:S(2)}) %copy-start) | copy-done | bytes 786456
  1.1 0.0 copy-start.1
  1.1 1.1 %copy-done.1 = bf16[3072,128]{1,0:T(8,128)(2,1)S(1)} copy-done((bf16[3072,128]{1,0:T(8,128)(2,1)S(1)}, bf16[3072,128]{1,0:T(8,128)(2,1)}, u32[]{:S(2)}) %copy-start.1) | copy-done | bytes 786456
  2.3 19.5 %solve_bins.1 = (bf16[3,64,512]{2,1,0:T(8,128)(2,1)S(1)}, bf16[3,64,512]{2,1,0:T(8,128)(2,1)S(1)}, f32[64,64]{1,0:T(8,128)S(1)}) custom-call(f32[1,768,3072]{2,1,0:T(8,128)} %x_hbm.1, f32[1,64,3072]{2,1,0:T(8,128)S(1)} %copy-done, bf16[3072,128]{1,0:T(8,128)(2,1)S(1)} %copy-done.1), custom_call_target="tpu_custom_call" | custom-call | tf_op jit(solution)/shard_map/solve_bins/pallas_call | solution.py:293
  21.8 1.4 %expand_bins.1 = f32[4,2,64,768]{3,2,1,0:T(8,128)} custom-call(bf16[3,64,512]{2,1,0:T(8,128)(2,1)S(1)} %get-tuple-element.8.eh, bf16[3,64,512]{2,1,0:T(8,128)(2,1)S(1)} %get-tuple-element.9.el, f32[64,64]{1,0:T(8,128)S(1)} %get-tuple-element.10.y), custom_call_target="tpu_custom_call" | custom-call | tf_op jit(solution)/shard_map/expand_bins/pallas_call | solution.py:322
Async XLA Ops:
  0.0 1.1 %copy-start = (f32[1,64,3072]{2,1,0:T(8,128)S(1)}, f32[1,64,3072]{2,1,0:T(8,128)}, u32[]{:S(2)}) copy-start(f32[1,64,3072]{2,1,0:T(8,128)} %up_hbm.1) | copy-start | bytes 2359300
  1.1 1.1 %copy-start.1 = (bf16[3072,128]{1,0:T(8,128)(2,1)S(1)}, bf16[3072,128]{1,0:T(8,128)(2,1)}, u32[]{:S(2)}) copy-start(bf16[3072,128]{1,0:T(8,128)(2,1)} %constant.2.clone.tab_hbm) | copy-start | bytes 2359300

commit v3 on v2

--- a/solution.py
+++ b/solution.py
@@ -11,7 +11,6 @@
 
 FREQ_DEV = 4
 PIECE = 1024
-AHEAD = 4
 ITERS = 2
 DAMPING = 0.5
 LANES = 128
@@ -104,28 +103,24 @@
     me, row = lax.axis_index("win"), lax.axis_index("row")
 
     n_piece, piece = tab.shape[0], tab.shape[1]
-    loads, ready = [], []
+    loads = []
     for ch in range(n_chunk):
+        lines = pl.ds(ch * width, width)
+        pairs = []
         for k in range(n_piece):
             span = pl.ds(k * piece, piece)
-            pairs = [(x_hbm.at[0, pl.ds(ch * width, width), span], xv.at[ch, k])]
             if ch == 0:
-                pairs = [(tab_hbm.at[span, :], tab.at[k]), (up_hbm.at[0, :, span], upv.at[k])] + pairs
-            for src, dst in pairs:
-                loads.append(pltpu.make_async_copy(src, dst, in_sem.at[len(loads)]))
-            ready.append(len(loads))
-    ahead = 3 * AHEAD
-    for load in loads[:ahead]:
+                pairs.append((tab_hbm.at[span, :], tab.at[k]))
+                pairs.append((up_hbm.at[0, :, span], upv.at[k]))
+            pairs.append((x_hbm.at[0, lines, span], xv.at[ch, k]))
+        loads.append(
+            [
+                pltpu.make_async_copy(src, dst, in_sem.at[ch, at])
+                for at, (src, dst) in enumerate(pairs)
+            ]
+        )
+    for load in loads[0] + loads[min(1, n_chunk - 1)] * (n_chunk > 1):
         load.start()
-    taken = [0]
-
-    def await_piece(number):
-        for at in range(taken[0], ready[number]):
-            loads[at].wait()
-        started = ahead + taken[0]
-        taken[0] = ready[number]
-        for load in loads[started : ahead + taken[0]]:
-            load.start()
 
     win_peers = [lax.rem(me + off, n_win) for off in range(1, n_win)]
     row_peers = [lax.rem(row + off, n_row) for off in range(1, n_row)]
@@ -162,8 +157,16 @@
 
     for ch in range(n_chunk):
         total = None
+        if ch:
+            for load in loads[ch]:
+                load.wait()
         for k in range(n_piece):
-            await_piece(ch * n_piece + k)
+            for load in loads[0][3 * k : 3 * k + 3] if ch == 0 else []:
+                load.wait()
+            if ch == 0 and k == 0:
+                for later in loads[2:]:
+                    for load in later:
+                        load.start()
             series = xv[ch, k]
             if ch == 0:
                 series = jnp.concatenate([series, upv[k]], axis=0)
@@ -307,7 +310,7 @@
             pltpu.VMEM((n_chunk, rows, 2 * width), BF16),
             pltpu.VMEM(g_shape, F32),
             pltpu.VMEM((n_row,) + g_shape, F32),
-            pltpu.SemaphoreType.DMA(((2 + n_chunk) * n_piece,)),
+            pltpu.SemaphoreType.DMA((n_chunk, 3 * n_piece)),
             pltpu.SemaphoreType.DMA((n_chunk + 1,)),
             pltpu.SemaphoreType.DMA((n_chunk + 1,)),
             pltpu.SemaphoreType.DMA((2,)),
@@ -317,7 +320,7 @@
             collective_id=0, has_side_effects=True, vmem_limit_bytes=50 * 1024 * 1024
         ),
         name="solve_bins",
-    )(downgoing, upgoing, table)
+    )(*[pltpu.with_memory_space_constraint(a, pltpu.MemorySpace.HBM) for a in (downgoing, upgoing, table)])
     out_shape = (FREQ_DEV, 2, n_virt, n_local)
     return pl.pallas_call(
         functools.partial(expand_kernel, (n_win, n_chunk, width, n_virt)),

time: 23.4 us -> 20.8 us (0.89)
  local copies, waits for them, and re-layouts: 2.27 us -> 0 us
  Pallas kernels: 20.9 us -> 20.6 us
    unnamed x4 -> x0, local copies, waits for them, and re-layouts: 2.27 us -> none
    pallas_call x1, Pallas kernels: 19.5 us -> 19.2 us  [body(): pl.pallas_call(functools.partial(solve_kernel, dims), out_shape=(ext, ext...]
where the time goes in v3:
time: 20.8 us; the launch traced here: 20.6 us
  Pallas kernels  20.6 us (99%)
    pallas_call x1, Pallas kernels, body(): pl.pallas_call(functools.partial(solve_kernel, dims), out_shape=(ext, ext...  19.2 us
    pallas_call x1, Pallas kernels, body(): pl.pallas_call(functools.partial(expand_kernel, (n_win, n_chunk, width, n...  1.4 us

profile of v3, /device:TPU:0, one launch (start us, length us, event | category | flops | bytes accessed | tf_op | source)
XLA Modules:
  0.0 20.6 jit_solution(16822773289044352909)
XLA Ops:
  0.0 19.2 %solve_bins.1 = (bf16[3,64,512]{2,1,0:T(8,128)(2,1)S(1)}, bf16[3,64,512]{2,1,0:T(8,128)(2,1)S(1)}, f32[64,64]{1,0:T(8,128)S(1)}) custom-call(f32[1,768,3072]{2,1,0:T(8,128)} %x_hbm.1, f32[1,64,3072]{2,1,0:T(8,128)} %up_hbm.1, bf16[3072,128]{1,0:T(8,128)(2,1)} %constant.2.clone.tab_hbm), custom_call_target="tpu_custom_call" | custom-call | tf_op jit(solution)/shard_map/solve_bins/pallas_call | solution.py:296
  19.2 1.4 %expand_bins.1 = f32[4,2,64,768]{3,2,1,0:T(8,128)} custom-call(bf16[3,64,512]{2,1,0:T(8,128)(2,1)S(1)} %get-tuple-element.8.eh, bf16[3,64,512]{2,1,0:T(8,128)(2,1)S(1)} %get-tuple-element.9.el, f32[64,64]{1,0:T(8,128)S(1)} %get-tuple-element.10.y), custom_call_target="tpu_custom_call" | custom-call | tf_op jit(solution)/shard_map/expand_bins/pallas_call | solution.py:325

commit v4 on v3

--- a/solution.py
+++ b/solution.py
@@ -10,7 +10,8 @@
 from jax.sharding import PartitionSpec as P
 
 FREQ_DEV = 4
-PIECE = 1024
+PIECE = 1536
+AHEAD = 3
 ITERS = 2
 DAMPING = 0.5
 LANES = 128
@@ -38,10 +39,20 @@
     return lax.dot_general(first, second, (dims, ((), ())), preferred_element_type=F32)
 
 
-def accumulate(total, series, table):
-    m = series.shape[0]
-    head, tail = halves(series)
-    part = dot(jnp.concatenate([head, tail], axis=0), table, ((1,), (0,)))
+def split_into(dst, parts):
+    total = sum(part.shape[0] for part in parts)
+    at = 0
+    for part in parts:
+        m = part.shape[0]
+        head, tail = halves(part[...])
+        dst[at : at + m, :] = head
+        dst[total + at : total + at + m, :] = tail
+        at += m
+    return total
+
+
+def accumulate(total, m, split, table):
+    part = dot(split[: 2 * m, :], table, ((1,), (0,)))
     part = part[:m] + part[m:]
     return part if total is None else total + part
 
@@ -93,7 +104,7 @@
 
 def solve_kernel(
     dims, x_hbm, up_hbm, tab_hbm, eh_out, el_out, y_out,
-    xv, upv, tab, sbuf, ubuf, recv, urecv, eh, el, g_send, g_recv,
+    xv, upv, tab, split_a, split_b, sbuf, ubuf, recv, urecv, eh, el, g_send, g_recv,
     in_sem, send_sem, recv_sem, g_sem, out_sem,
 ):
     n_win, n_row, n_chunk, width, n_virt, n_chan = dims
@@ -103,24 +114,37 @@
     me, row = lax.axis_index("win"), lax.axis_index("row")
 
     n_piece, piece = tab.shape[0], tab.shape[1]
+    pair = (split_a, split_b)
+    n_piece, piece = tab.shape[0], tab.shape[1]
+    pair = (split_a, split_b)
+    order = [(ch, k) for ch in range(n_chunk) for k in range(n_piece)]
     loads = []
-    for ch in range(n_chunk):
-        lines = pl.ds(ch * width, width)
-        pairs = []
-        for k in range(n_piece):
-            span = pl.ds(k * piece, piece)
-            if ch == 0:
-                pairs.append((tab_hbm.at[span, :], tab.at[k]))
-                pairs.append((up_hbm.at[0, :, span], upv.at[k]))
-            pairs.append((x_hbm.at[0, lines, span], xv.at[ch, k]))
+    for ch, k in order:
+        span = pl.ds(k * piece, piece)
+        pairs = [(x_hbm.at[0, pl.ds(ch * width, width), span], xv.at[ch, k])]
+        if ch == 0:
+            pairs = [(tab_hbm.at[span, :], tab.at[k])] + pairs + [(up_hbm.at[0, :, span], upv.at[k])]
         loads.append(
             [
-                pltpu.make_async_copy(src, dst, in_sem.at[ch, at])
+                pltpu.make_async_copy(src, dst, in_sem.at[len(loads), at])
                 for at, (src, dst) in enumerate(pairs)
             ]
         )
-    for load in loads[0] + loads[min(1, n_chunk - 1)] * (n_chunk > 1):
-        load.start()
+
+    def start(number):
+        for load in loads[number] if number < len(loads) else []:
+            load.start()
+
+    def split(number):
+        for load in loads[number]:
+            load.wait()
+        start(number + AHEAD)
+        ch, k = order[number]
+        parts = [xv.at[ch, k]] + ([upv.at[k]] if ch == 0 else [])
+        return split_into(pair[number % 2], parts)
+
+    for number in range(AHEAD):
+        start(number)
 
     win_peers = [lax.rem(me + off, n_win) for off in range(1, n_win)]
     row_peers = [lax.rem(row + off, n_row) for off in range(1, n_row)]
@@ -155,22 +179,14 @@
         part = ref.at[:, pl.ds(0, (n_win - 1) * slab), :]
         pltpu.make_async_copy(part, part, sem).wait()
 
-    for ch in range(n_chunk):
-        total = None
-        if ch:
-            for load in loads[ch]:
-                load.wait()
-        for k in range(n_piece):
-            for load in loads[0][3 * k : 3 * k + 3] if ch == 0 else []:
-                load.wait()
-            if ch == 0 and k == 0:
-                for later in loads[2:]:
-                    for load in later:
-                        load.start()
-            series = xv[ch, k]
-            if ch == 0:
-                series = jnp.concatenate([series, upv[k]], axis=0)
-            total = accumulate(total, series, tab[k])
+    lines = split(0)
+    total = None
+    for number, (ch, k) in enumerate(order):
+        later = split(number + 1) if number + 1 < len(order) else None
+        total = accumulate(total, lines, pair[number % 2], tab[k])
+        lines = later
+        if k + 1 < n_piece:
+            continue
         put(sbuf.at[ch], by_bin(total[:width]))
         if ch == 0:
             put(ubuf, by_bin(total[width:]))
@@ -178,6 +194,7 @@
         share(sbuf.at[ch], recv.at[ch], ch)
         if ch == 0:
             share(ubuf, urecv, n_chunk)
+        total = None
 
     gram = None
     stores = []
@@ -302,6 +319,8 @@
             pltpu.VMEM((n_chunk, n_piece, width, piece), F32),
             pltpu.VMEM((n_piece, n_virt, piece), F32),
             pltpu.VMEM((n_piece, piece, table.shape[1]), BF16),
+            pltpu.VMEM((2 * (width + n_virt), piece), BF16),
+            pltpu.VMEM((2 * (width + n_virt), piece), BF16),
             pltpu.VMEM((n_chunk, width // LANES, rows, LANES), F32),
             pltpu.VMEM((v_pad // LANES, rows, LANES), F32),
             pltpu.VMEM((n_chunk, width // LANES, rows, LANES), F32),
@@ -310,7 +329,7 @@
             pltpu.VMEM((n_chunk, rows, 2 * width), BF16),
             pltpu.VMEM(g_shape, F32),
             pltpu.VMEM((n_row,) + g_shape, F32),
-            pltpu.SemaphoreType.DMA((n_chunk, 3 * n_piece)),
+            pltpu.SemaphoreType.DMA((n_chunk * n_piece, 3)),
             pltpu.SemaphoreType.DMA((n_chunk + 1,)),
             pltpu.SemaphoreType.DMA((n_chunk + 1,)),
             pltpu.SemaphoreType.DMA((2,)),

time: 20.8 us -> 22.5 us (1.082)
  Pallas kernels: 20.6 us -> 22.3 us
    pallas_call x1, Pallas kernels: 19.2 us -> 20.9 us  [body(): pl.pallas_call(functools.partial(solve_kernel, dims), out_shape=(ext, ext...]
where the time goes in v4:
time: 22.5 us; the launch traced here: 22.3 us
  Pallas kernels  22.3 us (99%)
    pallas_call x1, Pallas kernels, body(): pl.pallas_call(functools.partial(solve_kernel, dims), out_shape=(ext, ext...  20.9 us
    pallas_call x1, Pallas kernels, body(): pl.pallas_call(functools.partial(expand_kernel, (n_win, n_chunk, width, n...  1.41 us

profile of v4, /device:TPU:0, one launch (start us, length us, event | category | flops | bytes accessed | tf_op | source)
XLA Modules:
  0.0 22.3 jit_solution(17354860092198246308)
XLA Ops:
  0.0 20.9 %solve_bins.1 = (bf16[3,64,512]{2,1,0:T(8,128)(2,1)S(1)}, bf16[3,64,512]{2,1,0:T(8,128)(2,1)S(1)}, f32[64,64]{1,0:T(8,128)S(1)}) custom-call(f32[1,768,3072]{2,1,0:T(8,128)} %x_hbm.1, f32[1,64,3072]{2,1,0:T(8,128)} %up_hbm.1, bf16[3072,128]{1,0:T(8,128)(2,1)} %constant.2.clone.tab_hbm), custom_call_target="tpu_custom_call" | custom-call | tf_op jit(solution)/shard_map/solve_bins/pallas_call | solution.py:313
  20.9 1.4 %expand_bins.1 = f32[4,2,64,768]{3,2,1,0:T(8,128)} custom-call(bf16[3,64,512]{2,1,0:T(8,128)(2,1)S(1)} %get-tuple-element.8.eh, bf16[3,64,512]{2,1,0:T(8,128)(2,1)S(1)} %get-tuple-element.9.el, f32[64,64]{1,0:T(8,128)S(1)} %get-tuple-element.10.y), custom_call_target="tpu_custom_call" | custom-call | tf_op jit(solution)/shard_map/expand_bins/pallas_call | solution.py:344

commit v5 on v3

--- a/solution.py
+++ b/solution.py
@@ -11,6 +11,7 @@
 
 FREQ_DEV = 4
 PIECE = 1024
+STEP = 256
 ITERS = 2
 DAMPING = 0.5
 LANES = 128
@@ -38,12 +39,17 @@
     return lax.dot_general(first, second, (dims, ((), ())), preferred_element_type=F32)
 
 
-def accumulate(total, series, table):
-    m = series.shape[0]
-    head, tail = halves(series)
-    part = dot(jnp.concatenate([head, tail], axis=0), table, ((1,), (0,)))
-    part = part[:m] + part[m:]
-    return part if total is None else total + part
+def accumulate(total, parts, table):
+    for at in range(0, table.shape[0], STEP):
+        span = slice(at, at + STEP)
+        series = [part[:, span] for part in parts]
+        series = jnp.concatenate(series, axis=0) if len(series) > 1 else series[0]
+        m = series.shape[0]
+        head, tail = halves(series)
+        weights = table[span, :]
+        part = dot(head, weights, ((1,), (0,))) + dot(tail, weights, ((1,), (0,)))
+        total = part if total is None else total + part
+    return total
 
 
 def by_bin(total):
@@ -167,10 +173,8 @@
                 for later in loads[2:]:
                     for load in later:
                         load.start()
-            series = xv[ch, k]
-            if ch == 0:
-                series = jnp.concatenate([series, upv[k]], axis=0)
-            total = accumulate(total, series, tab[k])
+            parts = [xv.at[ch, k]] + ([upv.at[k]] if ch == 0 else [])
+            total = accumulate(total, parts, tab.at[k])
         put(sbuf.at[ch], by_bin(total[:width]))
         if ch == 0:
             put(ubuf, by_bin(total[width:]))
@@ -256,18 +260,23 @@
 def expand_kernel(dims, eh, el, y, out_hbm, ov, sem):
     n_win, n_chunk, width, n_virt = dims
     block = 2 * n_win
+    rows = FREQ_DEV * block
+    row_id = lax.broadcasted_iota(jnp.int32, (rows, FREQ_DEV * n_virt), 0) // block
+    col_id = lax.broadcasted_iota(jnp.int32, (rows, FREQ_DEV * n_virt), 1) // n_virt
+    coef = jnp.where(row_id == col_id, jnp.concatenate([y[...]] * FREQ_DEV, axis=1), 0.0).T
+    head, tail = halves(coef)
+    coef = jnp.concatenate([head, tail, head], axis=1)
     stores = []
-    for f in range(FREQ_DEV):
-        own = slice(f * block, (f + 1) * block)
-        head, tail = halves(y[own, :])
-        coef = jnp.concatenate([head, tail, head], axis=0)
-        for ch in range(n_chunk):
-            big = eh[ch, own, :]
-            part = dot(coef, jnp.concatenate([big, big, el[ch, own, :]], axis=0), ((0,), (0,)))
-            span = slice(ch * width, (ch + 1) * width)
-            ov[f, 0, :, span] = part[:, :width]
-            ov[f, 1, :, span] = part[:, width:]
-        store = pltpu.make_async_copy(ov.at[f], out_hbm.at[f], sem.at[f])
+    for ch in range(n_chunk):
+        big = eh[ch]
+        part = dot(coef, jnp.concatenate([big, big, el[ch]], axis=0), ((1,), (0,)))
+        span = slice(ch * width, (ch + 1) * width)
+        for f in range(FREQ_DEV):
+            own = slice(f * n_virt, (f + 1) * n_virt)
+            ov[f, 0, :, span] = part[own, :width]
+            ov[f, 1, :, span] = part[own, width:]
+        lanes = pl.ds(ch * width, width)
+        store = pltpu.make_async_copy(ov.at[:, :, :, lanes], out_hbm.at[:, :, :, lanes], sem.at[ch])
         store.start()
         stores.append(store)
     for store in stores:
@@ -327,7 +336,7 @@
         out_shape=jax.ShapeDtypeStruct(out_shape, F32),
         in_specs=[vmem_spec] * 3,
         out_specs=any_spec,
-        scratch_shapes=[pltpu.VMEM(out_shape, F32), pltpu.SemaphoreType.DMA((FREQ_DEV,))],
+        scratch_shapes=[pltpu.VMEM(out_shape, F32), pltpu.SemaphoreType.DMA((n_chunk,))],
         compiler_params=pltpu.CompilerParams(vmem_limit_bytes=50 * 1024 * 1024),
         name="expand_bins",
     )(eh, el, y)

time: 20.8 us -> 20.7 us (level)
    pallas_call x1, Pallas kernels: 19.2 us -> 18.9 us  [body(): pl.pallas_call(functools.partial(solve_kernel, dims), out_shape=(ext, ext...]
    pallas_call x1, Pallas kernels: 1.4 us -> 1.65 us  [body(): pl.pallas_call(functools.partial(expand_kernel, (n_win, n_chunk, width, n...]
where the time goes in v5:
time: 20.7 us; the launch traced here: 20.6 us
  Pallas kernels  20.6 us (100%)
    pallas_call x1, Pallas kernels, body(): pl.pallas_call(functools.partial(solve_kernel, dims), out_shape=(ext, ext...  18.9 us
    pallas_call x1, Pallas kernels, body(): pl.pallas_call(functools.partial(expand_kernel, (n_win, n_chunk, width, n...  1.65 us

profile of v5, /device:TPU:0, one launch (start us, length us, event | category | flops | bytes accessed | tf_op | source)
XLA Modules:
  0.0 20.6 jit_solution(13162515053365538878)
XLA Ops:
  0.0 18.9 %solve_bins.1 = (bf16[3,64,512]{2,1,0:T(8,128)(2,1)S(1)}, bf16[3,64,512]{2,1,0:T(8,128)(2,1)S(1)}, f32[64,64]{1,0:T(8,128)S(1)}) custom-call(f32[1,768,3072]{2,1,0:T(8,128)} %x_hbm.1, f32[1,64,3072]{2,1,0:T(8,128)} %up_hbm.1, bf16[3072,128]{1,0:T(8,128)(2,1)} %constant.2.clone.tab_hbm), custom_call_target="tpu_custom_call" | custom-call | tf_op jit(solution)/shard_map/solve_bins/pallas_call | solution.py:305
  18.9 1.6 %expand_bins.1 = f32[4,2,64,768]{3,2,1,0:T(8,128)} custom-call(bf16[3,64,512]{2,1,0:T(8,128)(2,1)S(1)} %get-tuple-element.8.eh, bf16[3,64,512]{2,1,0:T(8,128)(2,1)S(1)} %get-tuple-element.9.el, f32[64,64]{1,0:T(8,128)S(1)} %get-tuple-element.10.y), custom_call_target="tpu_custom_call" | custom-call | tf_op jit(solution)/shard_map/expand_bins/pallas_call | solution.py:334

commit v6 on v3

--- a/solution.py
+++ b/solution.py
@@ -11,6 +11,7 @@
 
 FREQ_DEV = 4
 PIECE = 1024
+STEP = 256
 ITERS = 2
 DAMPING = 0.5
 LANES = 128
@@ -38,12 +39,17 @@
     return lax.dot_general(first, second, (dims, ((), ())), preferred_element_type=F32)
 
 
-def accumulate(total, series, table):
-    m = series.shape[0]
-    head, tail = halves(series)
-    part = dot(jnp.concatenate([head, tail], axis=0), table, ((1,), (0,)))
-    part = part[:m] + part[m:]
-    return part if total is None else total + part
+def accumulate(total, parts, table):
+    for at in range(0, table.shape[0], STEP):
+        span = slice(at, at + STEP)
+        series = [part[:, span] for part in parts]
+        series = jnp.concatenate(series, axis=0) if len(series) > 1 else series[0]
+        m = series.shape[0]
+        head, tail = halves(series)
+        weights = table[span, :]
+        part = dot(head, weights, ((1,), (0,))) + dot(tail, weights, ((1,), (0,)))
+        total = part if total is None else total + part
+    return total
 
 
 def by_bin(total):
@@ -93,7 +99,7 @@
 
 def solve_kernel(
     dims, x_hbm, up_hbm, tab_hbm, eh_out, el_out, y_out,
-    xv, upv, tab, sbuf, ubuf, recv, urecv, eh, el, g_send, g_recv,
+    xv, upv, tab, sbuf, recv, eh, el, g_send, g_recv,
     in_sem, send_sem, recv_sem, g_sem, out_sem,
 ):
     n_win, n_row, n_chunk, width, n_virt, n_chan = dims
@@ -119,7 +125,7 @@
                 for at, (src, dst) in enumerate(pairs)
             ]
         )
-    for load in loads[0] + loads[min(1, n_chunk - 1)] * (n_chunk > 1):
+    for load in loads[0]:
         load.start()
 
     win_peers = [lax.rem(me + off, n_win) for off in range(1, n_win)]
@@ -129,6 +135,11 @@
         pl.semaphore_signal(barrier, inc=1, device_id={"win": peer}, device_id_type=MESH)
     for peer in row_peers:
         pl.semaphore_signal(barrier, inc=1, device_id={"row": peer}, device_id_type=MESH)
+
+    n_sub = width // LANES
+
+    def slabs(buf, ch):
+        return buf.at[ch, pl.ds(0, buf.shape[1] if ch == 0 else n_sub)]
 
     def share(src, dst, at):
         own = pl.ds(pl.multiple_of(me * slab, slab), slab)
@@ -144,11 +155,11 @@
             ).start()
 
     def put(dst, value):
-        for sub in range(dst.shape[0]):
+        for sub in range(value.shape[1] // LANES):
             dst[sub] = value[:, sub * LANES : (sub + 1) * LANES]
 
-    def gather(src, number):
-        parts = [src[sub, pl.ds(number, n_win, stride=slab), :] for sub in range(src.shape[0])]
+    def gather(src, number, subs):
+        parts = [src[sub, pl.ds(number, n_win, stride=slab), :] for sub in subs]
         return jnp.concatenate(parts, axis=1) if len(parts) > 1 else parts[0]
 
     def await_all(ref, sem):
@@ -163,30 +174,26 @@
         for k in range(n_piece):
             for load in loads[0][3 * k : 3 * k + 3] if ch == 0 else []:
                 load.wait()
-            if ch == 0 and k == 0:
-                for later in loads[2:]:
+            if ch == 0:
+                until = k + 2 if k + 1 < n_piece else n_chunk
+                for later in loads[k + 1 : until]:
                     for load in later:
                         load.start()
-            series = xv[ch, k]
-            if ch == 0:
-                series = jnp.concatenate([series, upv[k]], axis=0)
-            total = accumulate(total, series, tab[k])
-        put(sbuf.at[ch], by_bin(total[:width]))
+            parts = [xv.at[ch, k]] + ([upv.at[k]] if ch == 0 else [])
+            total = accumulate(total, parts, tab.at[k])
+        put(sbuf.at[ch], by_bin(total))
         if ch == 0:
-            put(ubuf, by_bin(total[width:]))
             pl.semaphore_wait(barrier, n_win + n_row - 2)
-        share(sbuf.at[ch], recv.at[ch], ch)
-        if ch == 0:
-            share(ubuf, urecv, n_chunk)
+        share(slabs(sbuf, ch), slabs(recv, ch), ch)
 
     gram = None
     stores = []
     for ch in range(n_chunk):
-        await_all(recv.at[ch], recv_sem.at[ch])
+        await_all(slabs(recv, ch), recv_sem.at[ch])
         left, right = [], []
         for f in range(FREQ_DEV):
-            real = gather(recv.at[ch], 2 * f)
-            imag = gather(recv.at[ch], 2 * f + 1)
+            real = gather(recv.at[ch], 2 * f, range(n_sub))
+            imag = gather(recv.at[ch], 2 * f + 1, range(n_sub))
             left += [real, imag]
             right += [-imag, real]
         ext = jnp.concatenate(
@@ -227,11 +234,14 @@
             device_id={"row": peer},
             device_id_type=MESH,
         ).start()
-    await_all(urecv, recv_sem.at[n_chunk])
     rhs = jnp.concatenate(
-        [gather(urecv, number) for number in range(slab)], axis=0
+        [gather(recv.at[0], number, range(n_sub, recv.shape[1])) for number in range(slab)], axis=0
     ) / math.sqrt(n_chan)
     rhs = rhs[:, :n_virt]
+    for ch in range(n_chunk):
+        await_all(slabs(recv, ch), send_sem.at[ch])
+    for store in stores:
+        store.wait()
     if n_row > 1:
         part = g_recv.at[pl.ds(0, n_row - 1)]
         pltpu.make_async_copy(part, part, g_sem.at[1]).wait()
@@ -246,11 +256,6 @@
     if n_row > 1:
         part = g_recv.at[pl.ds(0, n_row - 1)]
         pltpu.make_async_copy(part, part, g_sem.at[0]).wait()
-    for ch in range(n_chunk):
-        await_all(recv.at[ch], send_sem.at[ch])
-    await_all(urecv, send_sem.at[n_chunk])
-    for store in stores:
-        store.wait()
 
 
 def expand_kernel(dims, eh, el, y, out_hbm, ov, sem):
@@ -302,17 +307,15 @@
             pltpu.VMEM((n_chunk, n_piece, width, piece), F32),
             pltpu.VMEM((n_piece, n_virt, piece), F32),
             pltpu.VMEM((n_piece, piece, table.shape[1]), BF16),
-            pltpu.VMEM((n_chunk, width // LANES, rows, LANES), F32),
-            pltpu.VMEM((v_pad // LANES, rows, LANES), F32),
-            pltpu.VMEM((n_chunk, width // LANES, rows, LANES), F32),
-            pltpu.VMEM((v_pad // LANES, rows, LANES), F32),
+            pltpu.VMEM((n_chunk, (width + v_pad) // LANES, rows, LANES), F32),
+            pltpu.VMEM((n_chunk, (width + v_pad) // LANES, rows, LANES), F32),
             pltpu.VMEM((n_chunk, rows, 2 * width), BF16),
             pltpu.VMEM((n_chunk, rows, 2 * width), BF16),
             pltpu.VMEM(g_shape, F32),
             pltpu.VMEM((n_row,) + g_shape, F32),
             pltpu.SemaphoreType.DMA((n_chunk, 3 * n_piece)),
-            pltpu.SemaphoreType.DMA((n_chunk + 1,)),
-            pltpu.SemaphoreType.DMA((n_chunk + 1,)),
+            pltpu.SemaphoreType.DMA((n_chunk,)),
+            pltpu.SemaphoreType.DMA((n_chunk,)),
             pltpu.SemaphoreType.DMA((2,)),
             pltpu.SemaphoreType.DMA((2 * n_chunk,)),
         ],

time: 20.8 us -> 20.4 us (0.981)
  Pallas kernels: 20.6 us -> 20.2 us
    pallas_call x1, Pallas kernels: 19.2 us -> 18.8 us  [body(): pl.pallas_call(functools.partial(solve_kernel, dims), out_shape=(ext, ext...]
where the time goes in v6:
time: 20.4 us; the launch traced here: 20.3 us
  Pallas kernels  20.2 us (99%)
    pallas_call x1, Pallas kernels, body(): pl.pallas_call(functools.partial(solve_kernel, dims), out_shape=(ext, ext...  18.8 us
    pallas_call x1, Pallas kernels, body(): pl.pallas_call(functools.partial(expand_kernel, (n_win, n_chunk, width, n...  1.4 us

profile of v6, /device:TPU:0, one launch (start us, length us, event | category | flops | bytes accessed | tf_op | source)
XLA Modules:
  0.0 20.3 jit_solution(12166505047303826725)
XLA Ops:
  0.0 18.8 %solve_bins.1 = (bf16[3,64,512]{2,1,0:T(8,128)(2,1)S(1)}, bf16[3,64,512]{2,1,0:T(8,128)(2,1)S(1)}, f32[64,64]{1,0:T(8,128)S(1)}) custom-call(f32[1,768,3072]{2,1,0:T(8,128)} %x_hbm.1, f32[1,64,3072]{2,1,0:T(8,128)} %up_hbm.1, bf16[3072,128]{1,0:T(8,128)(2,1)} %constant.2.clone.tab_hbm), custom_call_target="tpu_custom_call" | custom-call | tf_op jit(solution)/shard_map/solve_bins/pallas_call | solution.py:301
  18.9 1.4 %expand_bins.1 = f32[4,2,64,768]{3,2,1,0:T(8,128)} custom-call(bf16[3,64,512]{2,1,0:T(8,128)(2,1)S(1)} %get-tuple-element.8.eh, bf16[3,64,512]{2,1,0:T(8,128)(2,1)S(1)} %get-tuple-element.9.el, f32[64,64]{1,0:T(8,128)S(1)} %get-tuple-element.10.y), custom_call_target="tpu_custom_call" | custom-call | tf_op jit(solution)/shard_map/expand_bins/pallas_call | solution.py:328

commit v7 on v6

--- a/solution.py
+++ b/solution.py
@@ -284,7 +284,7 @@
     n_virt = upgoing.shape[1]
     n_win, n_row = lax.axis_size("win"), lax.axis_size("row")
     n_chan = n_local * n_row
-    width = 256 if n_local % 256 == 0 else 128
+    width = next(w for w in (384, 256, 128) if n_local % w == 0)
     n_chunk = n_local // width
     piece = PIECE if n_samples % PIECE == 0 else n_samples
     n_piece = n_samples // piece

time: 20.4 us -> 21.3 us (1.044)
  Pallas kernels: 20.2 us -> 21.1 us
    pallas_call x1, Pallas kernels: 18.8 us -> 19.7 us  [body(): pl.pallas_call(functools.partial(solve_kernel, dims), out_shape=(ext, ext...]
where the time goes in v7:
time: 21.3 us; the launch traced here: 21.1 us
  Pallas kernels  21.1 us (99%)
    pallas_call x1, Pallas kernels, body(): pl.pallas_call(functools.partial(solve_kernel, dims), out_shape=(ext, ext...  19.7 us
    pallas_call x1, Pallas kernels, body(): pl.pallas_call(functools.partial(expand_kernel, (n_win, n_chunk, width, n...  1.41 us

profile of v7, /device:TPU:0, one launch (start us, length us, event | category | flops | bytes accessed | tf_op | source)
XLA Modules:
  0.0 21.1 jit_solution(1624984307900170614)
XLA Ops:
  0.0 19.7 %solve_bins.1 = (bf16[2,64,768]{2,1,0:T(8,128)(2,1)S(1)}, bf16[2,64,768]{2,1,0:T(8,128)(2,1)S(1)}, f32[64,64]{1,0:T(8,128)S(1)}) custom-call(f32[1,768,3072]{2,1,0:T(8,128)} %x_hbm.1, f32[1,64,3072]{2,1,0:T(8,128)} %up_hbm.1, bf16[3072,128]{1,0:T(8,128)(2,1)} %constant.2.clone.tab_hbm), custom_call_target="tpu_custom_call" | custom-call | tf_op jit(solution)/shard_map/solve_bins/pallas_call | solution.py:301
  19.7 1.4 %expand_bins.1 = f32[4,2,64,768]{3,2,1,0:T(8,128)} custom-call(bf16[2,64,768]{2,1,0:T(8,128)(2,1)S(1)} %get-tuple-element.8.eh, bf16[2,64,768]{2,1,0:T(8,128)(2,1)S(1)} %get-tuple-element.9.el, f32[64,64]{1,0:T(8,128)S(1)} %get-tuple-element.10.y), custom_call_target="tpu_custom_call" | custom-call | tf_op jit(solution)/shard_map/expand_bins/pallas_call | solution.py:328

commit v8 on v7

--- a/solution.py
+++ b/solution.py
@@ -284,7 +284,7 @@
     n_virt = upgoing.shape[1]
     n_win, n_row = lax.axis_size("win"), lax.axis_size("row")
     n_chan = n_local * n_row
-    width = next(w for w in (384, 256, 128) if n_local % w == 0)
+    width = 128
     n_chunk = n_local // width
     piece = PIECE if n_samples % PIECE == 0 else n_samples
     n_piece = n_samples // piece

time: 21.3 us -> 19.9 us (0.934)
  Pallas kernels: 21.1 us -> 19.7 us
    pallas_call x1, Pallas kernels: 19.7 us -> 18.3 us  [body(): pl.pallas_call(functools.partial(solve_kernel, dims), out_shape=(ext, ext...]
where the time goes in v8:
time: 19.9 us; the launch traced here: 19.7 us
  Pallas kernels  19.7 us (99%)
    pallas_call x1, Pallas kernels, body(): pl.pallas_call(functools.partial(solve_kernel, dims), out_shape=(ext, ext...  18.3 us
    pallas_call x1, Pallas kernels, body(): pl.pallas_call(functools.partial(expand_kernel, (n_win, n_chunk, width, n...  1.41 us

profile of v8, /device:TPU:0, one launch (start us, length us, event | category | flops | bytes accessed | tf_op | source)
XLA Modules:
  0.0 19.7 jit_solution(15350265154868202501)
XLA Ops:
  0.0 18.3 %solve_bins.1 = (bf16[6,64,256]{2,1,0:T(8,128)(2,1)S(1)}, bf16[6,64,256]{2,1,0:T(8,128)(2,1)S(1)}, f32[64,64]{1,0:T(8,128)S(1)}) custom-call(f32[1,768,3072]{2,1,0:T(8,128)} %x_hbm.1, f32[1,64,3072]{2,1,0:T(8,128)} %up_hbm.1, bf16[3072,128]{1,0:T(8,128)(2,1)} %constant.2.clone.tab_hbm), custom_call_target="tpu_custom_call" | custom-call | tf_op jit(solution)/shard_map/solve_bins/pallas_call | solution.py:301
  18.3 1.4 %expand_bins.1 = f32[4,2,64,768]{3,2,1,0:T(8,128)} custom-call(bf16[6,64,256]{2,1,0:T(8,128)(2,1)S(1)} %get-tuple-element.8.eh, bf16[6,64,256]{2,1,0:T(8,128)(2,1)S(1)} %get-tuple-element.9.el, f32[64,64]{1,0:T(8,128)S(1)} %get-tuple-element.10.y), custom_call_target="tpu_custom_call" | custom-call | tf_op jit(solution)/shard_map/expand_bins/pallas_call | solution.py:328
